TPU v7x, 512 devices: a whole 4x8x8 slice. The times are simulated.
512 devices in a mesh: seq: 128 (over z_lo, x, y), dp: 4 (over z_hi, core).
Axes of the slice: x: 4, y: 8, z: 8 (z_hi: 2, z_lo: 4; z = z_hi * 4 + z_lo), core: 2. Of those that a mesh axis runs over, the one named last changes fastest.
Arguments:
- byte_qkv: bfloat16 [4, 32768, 3072], P('dp', 'seq'), may hold values from -6 to 6
- patch_qkv: bfloat16 [4, 8192, 3072], P('dp', 'seq'), may hold values from -6 to 6
- patch_gain: float32 [3072], replicated, may hold values from 0.3 to 1.5
- out_grad: bfloat16 [4, 32768, 1024], P('dp', 'seq'), may hold values from -48 to 48
- patch_slot: int32 [4, 32768], P('dp', 'seq'), may hold values from 0 to 63, as said below
- lead: int32 [4, 128], P('dp', 'seq'), may hold values from 0 to 15, as said below
Outputs:
- byte_grad: bfloat16 [4, 32768, 3072], P('dp', 'seq')
- patch_grad: bfloat16 [4, 8192, 3072], P('dp', 'seq')
- gain_grad: float32 [3072], replicated
Inputs may be any that keep to these rules, and one draw needn't show every extreme that they name: Patches are runs of 1 to 31 bytes of a stream. A patch is owned by the device that holds its first byte; each device numbers the patches starting on it 0, 1, 2 and so on in order, and patch_slot gives each byte the number of its patch on the owning device. Every device holds the first byte of at least one patch. lead[s, d] bytes at the start of device d's run of stream s belong to the last patch that starts on device d - 1; lead[s, 0] = 0.
All inputs are finite; a program needn't handle non-finite values.
Results may differ from a plain program's by a relative error of at most 0.011.
Values may be sent and summed in bfloat16 or wider, within the bound.
A program may use at most 128 MiB of HBM per device.

v0:
```python
import math

import jax
import jax.numpy as jnp
from jax import lax
from jax.sharding import PartitionSpec as P

HEADS = 8
HEAD_DIM = 128
WIN = 512


def shifted(value, axis, steps):
    count = lax.axis_size(axis)
    initial, last = (max(0, -steps), min(count, count - steps))
    return lax.ppermute(value, axis, [(source, source + steps) for source in range(initial, last)])


def local(byte_qkv, patch_qkv, patch_gain, out_grad, patch_slot, lead):
    own_bytes = byte_qkv[0]
    patch_table = patch_qkv[0]
    cotangent = out_grad[0]
    slot_ids = patch_slot[0]
    row_count = own_bytes.shape[0]
    feature_count = cotangent.shape[1]
    capacity = patch_table.shape[0]
    first_pos = lax.axis_index("seq") * row_count
    reach_blocks = -(-WIN // row_count)
    inv_sqrt = 1.0 / math.sqrt(HEAD_DIM)
    local_rows = lax.broadcasted_iota(jnp.int32, (row_count,), 0)
    leading = local_rows < lead[0, 0]
    owned_slots = jnp.where(leading, -1, slot_ids)
    last_slot = jnp.max(owned_slots)
    last_row = lax.dynamic_slice_in_dim(patch_table, last_slot, 1, 0)
    prev_row = shifted(last_row, "seq", 1)
    slot_axis = lax.broadcasted_iota(jnp.int32, (row_count, capacity), 1)
    pick_rows = (slot_ids[:, None] == slot_axis).astype(jnp.bfloat16)
    patch_rows = jnp.dot(pick_rows, patch_table, preferred_element_type=jnp.float32)
    patch_rows = jnp.where(leading[:, None], prev_row.astype(jnp.float32), patch_rows)
    hidden = (patch_gain * patch_rows + own_bytes.astype(jnp.float32)).astype(jnp.bfloat16)
    queries = hidden[:, :feature_count]
    key_values = hidden[:, feature_count:]
    blocks = [key_values]
    arrived = shifted(key_values, "seq", 1)
    blocks.append(arrived)
    steps_back = 2
    arrived = shifted(key_values, "seq", steps_back)
    blocks.append(arrived)
    window = jnp.concatenate(blocks[::-1], axis=0)
    key_count = window.shape[0]
    query_pos = first_pos + local_rows
    key_pos = (
        first_pos - reach_blocks * row_count + lax.broadcasted_iota(jnp.int32, (key_count,), 0)
    )
    in_window = (
        (key_pos[None, :] <= query_pos[:, None])
        & (key_pos[None, :] > query_pos[:, None] - WIN)
        & (key_pos[None, :] >= 0)
    )
    query_parts = []
    key_parts = []
    value_parts = []
    max_list = []
    total_list = []
    delta_list = []
    for head_index in range(HEADS):
        low = head_index * HEAD_DIM
        query_head = queries[:, low : low + HEAD_DIM]
        cot_head = cotangent[:, low : low + HEAD_DIM]
        key_head = window[:, low : low + HEAD_DIM]
        value_head = window[:, feature_count + low : feature_count + low + HEAD_DIM]
        scores = (
            jnp.einsum("qe,ke->qk", query_head, key_head, preferred_element_type=jnp.float32)
            * inv_sqrt
        )
        scores = jnp.where(in_window, scores, -jnp.inf)
        row_max = jnp.max(scores, axis=1, keepdims=True)
        exponent = jnp.where(in_window, jnp.exp(scores - row_max), 0.0)
        row_total = jnp.sum(exponent, axis=1, keepdims=True)
        attn_prob = exponent / row_total
        prob_half = attn_prob.astype(jnp.bfloat16)
        value_parts.append(
            jnp.einsum("qk,qe->ke", prob_half, cot_head, preferred_element_type=jnp.float32)
        )
        prob_grad = jnp.einsum(
            "qe,ke->qk", cot_head, value_head, preferred_element_type=jnp.float32
        )
        row_delta = jnp.sum(attn_prob * prob_grad, axis=1, keepdims=True)
        score_grad = (attn_prob * (prob_grad - row_delta)).astype(jnp.bfloat16)
        query_parts.append(
            jnp.einsum("qk,ke->qe", score_grad, key_head, preferred_element_type=jnp.float32)
            * inv_sqrt
        )
        key_parts.append(
            jnp.einsum("qk,qe->ke", score_grad, query_head, preferred_element_type=jnp.float32)
            * inv_sqrt
        )
        max_list.append(row_max[:, 0])
        total_list.append(row_total[:, 0])
        delta_list.append(row_delta[:, 0])
    query_grad = jnp.concatenate(query_parts, axis=1)
    key_part = jnp.concatenate(key_parts, axis=1)
    value_part = jnp.concatenate(value_parts, axis=1)
    back_grads = jnp.concatenate([key_part, value_part], axis=1)
    own_grads = back_grads[key_count - row_count :]
    for steps_back in range(1, reach_blocks + 1):
        piece_first = (reach_blocks - steps_back) * row_count
        piece = back_grads[piece_first : piece_first + row_count]
        own_grads = own_grads + shifted(piece, "seq", -steps_back)
    hidden_grad = jnp.concatenate([query_grad, own_grads], axis=1)
    byte_grad = hidden_grad.astype(jnp.bfloat16)[None]
    lead_sum = jnp.sum(jnp.where(leading[:, None], hidden_grad, 0.0), axis=0, keepdims=True)
    from_next = shifted(lead_sum, "seq", -1)
    slot_column = lax.broadcasted_iota(jnp.int32, (capacity, row_count), 0)
    member = ((slot_ids[None, :] == slot_column) & jnp.logical_not(leading)[None, :]).astype(
        jnp.float32
    )
    slot_sums = jnp.dot(
        member, hidden_grad, precision=lax.Precision.HIGHEST, preferred_element_type=jnp.float32
    )
    slot_index = lax.broadcasted_iota(jnp.int32, (capacity, 1), 0)
    slot_sums = slot_sums + (slot_index == last_slot).astype(jnp.float32) * from_next
    patch_grad = (patch_gain * slot_sums).astype(jnp.bfloat16)[None]
    gain_term = jnp.sum(slot_sums * patch_table.astype(jnp.float32), axis=0)
    gain_grad = lax.psum(gain_term, ("seq", "dp")) / row_count
    return (byte_grad, patch_grad, gain_grad)


def solution(mesh):
    placed = (
        P("dp", "seq", None),
        P("dp", "seq", None),
        P(),
        P("dp", "seq", None),
        P("dp", "seq"),
        P("dp", "seq"),
    )
    return jax.shard_map(
        local,
        mesh=mesh,
        in_specs=placed,
        out_specs=(P("dp", "seq", None), P("dp", "seq", None), P()),
        check_vma=False,
    )
```

profile of v0, /device:TPU:1, one launch (start us, length us, event | category | flops | bytes accessed | tf_op | source)
XLA Modules:
  0.0 348.9 jit_solution(16617319942461404328)
XLA Ops:
  1.3 1.3 select_reduce_fusion.1
  4.5 0.8 dynamic-slice_bitcast_fusion
  5.4 4.0 %collective-permute-start = (bf16[1,3072]{1,0:T(2,128)(2,1)S(1)}, bf16[1,3072]{1,0:T(2,128)(2,1)S(1)}, u32[]{:S(2)}, u32[]{:S(2)}) collective-permute-start(bf16[1,3072]{1,0:T(2,128)(2,1)S(1)} %dynamic-slice_bitcast_fusion), channel_id=1, source_target_pairs={{0,4},{4,8},{8,12},{12,16},{16,20},{20,24},{24,28},{28,32},{32,36}... | collective-permute-start | bytes 18440 | tf_op jit(solution)/shard_map/ppermute | solution.py:16
  10.2 2.3 fusion
  12.6 4.6 %collective-permute-start.2 = (bf16[256,2048]{1,0:T(8,128)(2,1)S(1)}, bf16[256,2048]{1,0:T(8,128)(2,1)}, u32[]{:S(2)}, u32[]{:S(2)}) collective-permute-start(bf16[256,2048]{1,0:T(8,128)(2,1)S(1)} %slice.154), channel_id=1, source_target_pairs={{0,4},{4,8},{8,12},{12,16},{16,20},{20,24},{24,28},{28,32},{32,36}... | collective-permute-start | bytes 3145736 | tf_op jit(solution)/shard_map/ppermute | solution.py:16
  17.2 5.1 %collective-permute-start.1 = (bf16[256,2048]{1,0:T(8,128)(2,1)S(1)}, bf16[256,2048]{1,0:T(8,128)(2,1)}, u32[]{:S(2)}, u32[]{:S(2)}) collective-permute-start(bf16[256,2048]{1,0:T(8,128)(2,1)S(1)} %slice.154), channel_id=1, source_target_pairs={{0,8},{4,12},{8,16},{12,20},{16,24},{20,28},{24,32},{28,36},{32,40... | collective-permute-start | bytes 3145736 | tf_op jit(solution)/shard_map/ppermute | solution.py:16
  23.0 10.7 %collective-permute-done.2 = bf16[256,2048]{1,0:T(8,128)(2,1)} collective-permute-done((bf16[256,2048]{1,0:T(8,128)(2,1)S(1)}, bf16[256,2048]{1,0:T(8,128)(2,1)}, u32[]{:S(2)}, u32[]{:S(2)}) %collective-permute-start.2) | collective-permute-done | bytes 1048608 | tf_op jit(solution)/shard_map/ppermute | solution.py:16
  33.6 24.7 %collective-permute-done.1 = bf16[256,2048]{1,0:T(8,128)(2,1)} collective-permute-done((bf16[256,2048]{1,0:T(8,128)(2,1)S(1)}, bf16[256,2048]{1,0:T(8,128)(2,1)}, u32[]{:S(2)}, u32[]{:S(2)}) %collective-permute-start.1) | collective-permute-done | bytes 1048608 | tf_op jit(solution)/shard_map/ppermute | solution.py:16
  58.3 1.8 pad_maximum_fusion
  64.9 0.9 fusion.33
  65.8 1.4 multiply_reduce_fusion.1
  67.2 1.1 multiply_reduce_fusion.3
  68.3 1.1 multiply_reduce_fusion.2
  69.4 1.0 multiply_convert_fusion.6
  71.9 1.0 multiply_convert_fusion.1
  72.9 1.2 multiply_convert_fusion.3
  81.1 1.3 collective-permute-start.4
  82.4 1.3 collective-permute-start.3
  85.6 29.1 %collective-permute-done.4 = f32[256,2048]{1,0:T(8,128)S(1)} collective-permute-done((f32[256,2048]{1,0:T(8,128)S(1)}, f32[256,2048]{1,0:T(8,128)S(1)}, u32[]{:S(2)}, u32[]{:S(2)}) %collective-permute-start.4) | collective-permute-done | bytes 2097184 | tf_op jit(solution)/shard_map/ppermute | solution.py:16
  114.7 46.9 %collective-permute-done.3 = f32[256,2048]{1,0:T(8,128)S(1)} collective-permute-done((f32[256,2048]{1,0:T(8,128)S(1)}, f32[256,2048]{1,0:T(8,128)S(1)}, u32[]{:S(2)}, u32[]{:S(2)}) %collective-permute-start.3) | collective-permute-done | bytes 2097184 | tf_op jit(solution)/shard_map/ppermute | solution.py:16
  162.7 1.3 collective-permute-start.5
  164.5 44.3 %collective-permute-done.5 = f32[1,3072]{1,0:T(1,128)S(1)} collective-permute-done((f32[1,3072]{1,0:T(1,128)S(1)}, f32[1,3072]{1,0:T(1,128)S(1)}, u32[]{:S(2)}, u32[]{:S(2)}) %collective-permute-start.5) | collective-permute-done | bytes 12320 | tf_op jit(solution)/shard_map/ppermute | solution.py:16
  208.9 2.2 multiply_reduce_fusion
  211.1 137.2 %psum.7 = f32[3072]{0:T(1024)S(1)} all-reduce(f32[3072]{0:T(1024)S(1)} %get-tuple-element.20), channel_id=1, replica_groups=mesh['seq'=128,'dp'=4] {'seq','dp'}, use_global_device_ids=true, to_apply=%region_27.28 | all-reduce | flops 3072 | bytes 24576 | tf_op jit(solution)/shard_map/psum | solution.py:125
  (68 shorter events, 18.6 us)
Async XLA Ops:
  5.4 4.9 %collective-permute-start = (bf16[1,3072]{1,0:T(2,128)(2,1)S(1)}, bf16[1,3072]{1,0:T(2,128)(2,1)S(1)}, u32[]{:S(2)}, u32[]{:S(2)}) collective-permute-start(bf16[1,3072]{1,0:T(2,128)(2,1)S(1)} %dynamic-slice_bitcast_fusion), channel_id=1, source_target_pairs={{0,4},{4,8},{8,12},{12,16},{16,20},{20,24},{24,28},{28,32},{32,36}... | collective-permute-start | bytes 18440 | tf_op jit(solution)/shard_map/ppermute | solution.py:16
  12.6 21.1 %collective-permute-start.2 = (bf16[256,2048]{1,0:T(8,128)(2,1)S(1)}, bf16[256,2048]{1,0:T(8,128)(2,1)}, u32[]{:S(2)}, u32[]{:S(2)}) collective-permute-start(bf16[256,2048]{1,0:T(8,128)(2,1)S(1)} %slice.154), channel_id=1, source_target_pairs={{0,4},{4,8},{8,12},{12,16},{16,20},{20,24},{24,28},{28,32},{32,36}... | collective-permute-start | bytes 3145736 | tf_op jit(solution)/shard_map/ppermute | solution.py:16
  17.2 41.1 %collective-permute-start.1 = (bf16[256,2048]{1,0:T(8,128)(2,1)S(1)}, bf16[256,2048]{1,0:T(8,128)(2,1)}, u32[]{:S(2)}, u32[]{:S(2)}) collective-permute-start(bf16[256,2048]{1,0:T(8,128)(2,1)S(1)} %slice.154), channel_id=1, source_target_pairs={{0,8},{4,12},{8,16},{12,20},{16,24},{20,28},{24,32},{28,36},{32,40... | collective-permute-start | bytes 3145736 | tf_op jit(solution)/shard_map/ppermute | solution.py:16
  62.0 1.8 copy-start.1
  81.1 33.7 %collective-permute-start.4 = (f32[256,2048]{1,0:T(8,128)S(1)}, f32[256,2048]{1,0:T(8,128)S(1)}, u32[]{:S(2)}, u32[]{:S(2)}) collective-permute-start(f32[256,2048]{1,0:T(8,128)S(1)} %get-tuple-element.19), channel_id=1, source_target_pairs={{8,0},{12,4},{16,8},{20,12},{24,16},{28,20},{32,24},{36,28},{40,32... | collective-permute-start | bytes 6291464 | tf_op jit(solution)/shard_map/ppermute | solution.py:16
  82.4 79.3 %collective-permute-start.3 = (f32[256,2048]{1,0:T(8,128)S(1)}, f32[256,2048]{1,0:T(8,128)S(1)}, u32[]{:S(2)}, u32[]{:S(2)}) collective-permute-start(f32[256,2048]{1,0:T(8,128)S(1)} %get-tuple-element.18), channel_id=1, source_target_pairs={{4,0},{8,4},{12,8},{16,12},{20,16},{24,20},{28,24},{32,28},{36,32}... | collective-permute-start | bytes 6291464 | tf_op jit(solution)/shard_map/ppermute | solution.py:16
  162.7 46.1 %collective-permute-start.5 = (f32[1,3072]{1,0:T(1,128)S(1)}, f32[1,3072]{1,0:T(1,128)S(1)}, u32[]{:S(2)}, u32[]{:S(2)}) collective-permute-start(f32[1,3072]{1,0:T(1,128)S(1)} %bitcast.89), channel_id=1, source_target_pairs={{4,0},{8,4},{12,8},{16,12},{20,16},{24,20},{28,24},{32,28},{36,32}... | collective-permute-start | bytes 36872 | tf_op jit(solution)/shard_map/ppermute | solution.py:16
  164.0 44.8 %copy-start = (bf16[1,64,3072]{2,1,0:T(8,128)(2,1)S(1)}, bf16[1,64,3072]{2,1,0:T(8,128)(2,1)}, u32[]{:S(2)}) copy-start(bf16[1,64,3072]{2,1,0:T(8,128)(2,1)} %param.7) | copy-start | bytes 1179652
  164.1 44.8 %copy-start.2 = (f32[3072]{0:T(1024)S(1)}, f32[3072]{0:T(1024)}, u32[]{:S(2)}) copy-start(f32[3072]{0:T(1024)} %param.8) | copy-start | bytes 36868
  164.1 44.8 %copy-start.3 = (s32[1,256]{1,0:T(1,128)S(1)}, s32[1,256]{1,0:T(1,128)}, u32[]{:S(2)}) copy-start(s32[1,256]{1,0:T(1,128)} %param.10) | copy-start | bytes 3076
  164.5 46.6 %copy-start.4 = (bf16[1,256,3072]{2,1,0:T(8,128)(2,1)}, bf16[1,256,3072]{2,1,0:T(8,128)(2,1)S(1)}, u32[]{:S(2)}) copy-start(bf16[1,256,3072]{2,1,0:T(8,128)(2,1)S(1)} %bitcast_dynamic-update-slice_fusion) | copy-start | bytes 4718596
where the time goes:
time: 349 us
  waiting for transfers between devices  157 us (45%)
  blocking collectives  137 us (39%)
  matrix products  23.3 us (7%)
  starting transfers between devices  17.6 us (5%)
  other arithmetic  9.05 us (3%)
  between operations  3.69 us (1%)
    ppermute x6, waiting for transfers between devices, shifted(): lax.ppermute(value, axis, [(source, source + steps) for source in range(i...  157 us
    psum x1, blocking collectives, local(): gain_grad = lax.psum(gain_term, ('seq', 'dp')) / row_count  137 us
    ppermute x6, starting transfers between devices, shifted(): lax.ppermute(value, axis, [(source, source + steps) for source in range(i...  17.6 us
  transfers between devices with their start and end apart: 6, of which 6 were waited for; matrix products, arithmetic and copies ran while one was open for 1% of the time, Pallas kernels for 0%

commit v1 on v0

v1 whole, which is shorter than its diff:
```python
import functools
import math

import jax
import jax.numpy as jnp
from jax import lax
from jax.experimental import pallas as pl
from jax.experimental.pallas import tpu as pltpu
from jax.sharding import PartitionSpec as P

HEADS = 8
HD = 128
ROWS = 256
CAP = 64
N_SEQ = 128
MESH = pl.DeviceIdType.MESH
BF = jnp.bfloat16
F32 = jnp.float32

NEG = -1e9
SCALE = 1.0 / math.sqrt(HD)
SCALE2 = SCALE / math.log(2.0)
AHEAD = 3
LAG2 = 3
LAG3 = 5
LAG4 = 6
SLOTS = LAG2 + 1

K_Q, K_DO, K_KV, K_SA, K_SB, K_DKV, K_DQ, K_LS = range(8)


def nt(a, b):
    return lax.dot_general(a, b, (((1,), (1,)), ((), ())), preferred_element_type=F32)


def nn(a, b):
    return lax.dot_general(a, b, (((1,), (0,)), ((), ())), preferred_element_type=F32)


def tn(a, b):
    return lax.dot_general(a, b, (((0,), (0,)), ((), ())), preferred_element_type=F32)


def cols(block):
    return pl.ds(pl.multiple_of(block * HD, HD), HD)


def peer_groups(me, dp):
    y = lax.rem(me, 8)
    x = lax.rem(me // 8, 4)
    z_lo = me // 32
    z_hi = dp // 2
    core = lax.rem(dp, 2)
    along_z, along_xc, along_y = [], [], []
    for k in range(1, 8):
        z = lax.rem(z_hi * 4 + z_lo + k, 8)
        along_z.append(((lax.rem(z, 4) * 4 + x) * 8 + y, (z // 4) * 2 + core))
        p = lax.rem(x * 2 + core + k, 8)
        along_xc.append(((z_lo * 4 + p // 2) * 8 + y, z_hi * 2 + lax.rem(p, 2)))
        along_y.append(((z_lo * 4 + x) * 8 + lax.rem(y + k, 8), dp))
    return along_z, along_xc, along_y


def kernel(
    byte_ref,
    patch_ref,
    gain_ref,
    cot_ref,
    slot_ref,
    lead_ref,
    bg_ref,
    pg_ref,
    gg_ref,
    byte_v,
    tab_v,
    oh,
    mem,
    qdo_own,
    kv_own,
    qdo_nxt,
    kv_prv,
    dq_loc,
    dkv_loc,
    dq_snd,
    dkv_snd,
    dq_rcv,
    dkv_rcv,
    pbuf,
    dpbuf,
    sa_own,
    sa_nxt,
    sb_own,
    sb_rcv,
    prev_snd,
    prev_rcv,
    ls_snd,
    ls_rcv,
    last_col,
    ssum,
    out_b,
    out_p,
    g_acc,
    g_rcv,
    in_sem,
    do_sem,
    s_sem,
    r_sem,
    prev_sem,
    ob_sem,
    op_sem,
    gs_sem,
    gr_sem,
):
    me = lax.axis_index("seq")
    dp = lax.axis_index("dp")
    has_left = me > 0
    has_right = me < N_SEQ - 1
    left = (me - 1, dp)
    right = (me + 1, dp)
    groups = peer_groups(me, dp)

    barrier = pltpu.get_barrier_semaphore()

    @pl.when(has_left)
    def _():
        pl.semaphore_signal(barrier, inc=1, device_id=left, device_id_type=MESH)

    @pl.when(has_right)
    def _():
        pl.semaphore_signal(barrier, inc=1, device_id=right, device_id_type=MESH)

    for group in groups:
        for peer in group:
            pl.semaphore_signal(barrier, inc=1, device_id=peer, device_id_type=MESH)

    load_tab = pltpu.make_async_copy(patch_ref.at[0], tab_v.at[pl.ds(0, CAP)], in_sem.at[0])
    load_tab.start()
    load_byte = pltpu.make_async_copy(byte_ref.at[0], byte_v, in_sem.at[1])
    load_byte.start()

    def load_do(h):
        return pltpu.make_async_copy(cot_ref.at[0, :, cols(h)], qdo_own.at[h, 1], do_sem.at[h])

    for h in range(HEADS):
        load_do(h).start()

    lead = lead_ref[0, 0]
    slots = slot_ref[...]
    row_i = lax.broadcasted_iota(jnp.int32, (HD, ROWS), 0)
    lane_i = lax.broadcasted_iota(jnp.int32, (HD, ROWS), 1)
    pick = jnp.where(row_i == slots, 1.0, 0.0)
    oh[...] = jnp.transpose(pick).astype(BF)
    mem[...] = jnp.where(lane_i < lead, jnp.where(row_i == CAP, 1.0, 0.0), pick)[:80].astype(BF)
    last_col[...] = jnp.broadcast_to(pick[:CAP, ROWS - 1 : ROWS], (CAP, HD))
    tab_v[CAP:] = jnp.zeros((HD - CAP, 3 * HEADS * HD), BF)

    @pl.when(jnp.logical_not(has_left))
    def _():
        kv_prv[...] = jnp.zeros_like(kv_prv)
        dq_rcv[...] = jnp.zeros_like(dq_rcv)
        prev_rcv[...] = jnp.zeros_like(prev_rcv)
        sb_rcv[...] = jnp.full(sb_rcv.shape, NEG, F32)

    @pl.when(jnp.logical_not(has_right))
    def _():
        qdo_nxt[...] = jnp.zeros_like(qdo_nxt)
        dkv_rcv[...] = jnp.zeros_like(dkv_rcv)
        ls_rcv[...] = jnp.zeros_like(ls_rcv)
        sa_nxt[...] = jnp.ones_like(sa_nxt)

    load_tab.wait()
    load_byte.wait()

    def hidden_dst(part, h):
        return qdo_own.at[h, 0] if part == 0 else kv_own.at[h, part - 1]

    def make_hidden(h, carry):
        for part in range(3):
            cb = part * HEADS + h
            rows = nn(oh[...], tab_v[:, cols(cb)])
            prev_snd[cb] = rows[ROWS - 1 : ROWS]
            hidden = gain_ref[:, cols(cb)] * rows + byte_v[:, cols(cb)].astype(F32)
            hidden_dst(part, h)[...] = hidden.astype(BF)
        return carry

    lax.fori_loop(0, HEADS, make_hidden, 0)
    for h in range(HEADS):
        load_do(h).wait()

    neighbours = has_left.astype(jnp.int32) + has_right.astype(jnp.int32)
    pl.semaphore_wait(barrier, neighbours + 21)

    def remote(kind, h, src, dst, to):
        return pltpu.make_async_remote_copy(
            src_ref=src,
            dst_ref=dst,
            send_sem=s_sem.at[kind, h],
            recv_sem=r_sem.at[kind, h],
            device_id=to,
            device_id_type=MESH,
        )

    def c_q(h):
        return remote(K_Q, h, qdo_own.at[h, 0], qdo_nxt.at[h, 0], left)

    def c_do(h):
        return remote(K_DO, h, qdo_own.at[h, 1], qdo_nxt.at[h, 1], left)

    def c_kv(h):
        return remote(K_KV, h, kv_own.at[h], kv_prv.at[h], right)

    def c_sa(h):
        return remote(K_SA, h, sa_own.at[h], sa_nxt.at[h], left)

    def c_sb(h):
        return remote(K_SB, h, sb_own.at[h], sb_rcv.at[h], right)

    def c_dkv(h):
        return remote(K_DKV, h, dkv_snd.at[h], dkv_rcv.at[h], left)

    def c_dq(h):
        return remote(K_DQ, h, dq_snd.at[h], dq_rcv.at[h], right)

    def c_ls(h):
        return remote(K_LS, h, ls_snd.at[h], ls_rcv.at[h], left)

    c_prev = pltpu.make_async_remote_copy(
        src_ref=prev_snd,
        dst_ref=prev_rcv,
        send_sem=prev_sem.at[0],
        recv_sem=prev_sem.at[1],
        device_id=right,
        device_id_type=MESH,
    )

    @pl.when(has_right)
    def _():
        c_prev.start()

    @pl.when(has_left)
    def _():
        for h in range(AHEAD):
            c_do(h).start()
        c_prev.wait_recv()

    lead_rows = lax.broadcasted_iota(jnp.int32, (16, HD), 0) < lead

    def fix_hidden(h, carry):
        for part in range(3):
            cb = part * HEADS + h
            dst = hidden_dst(part, h)
            fixed = gain_ref[:, cols(cb)] * prev_rcv[cb] + byte_v[:16, cols(cb)].astype(F32)
            dst[:16] = jnp.where(lead_rows, fixed, dst[:16].astype(F32)).astype(BF)
        return carry

    lax.fori_loop(0, HEADS, fix_hidden, 0)

    def send_inputs(h, with_do=True):
        @pl.when(has_left)
        def _():
            c_q(h).start()
            if with_do:
                c_do(h).start()

        @pl.when(has_right)
        def _():
            c_kv(h).start()

    for h in range(AHEAD):
        send_inputs(h, False)

    def phase1(h):
        slot = lax.rem(h, SLOTS)

        @pl.when(has_left)
        def _():
            c_kv(h).wait_recv()

        @pl.when(has_right)
        def _():
            c_q(h).wait_recv()
            c_do(h).wait_recv()

        key_i = lax.broadcasted_iota(jnp.int32, (ROWS, ROWS), 0)
        query_i = lax.broadcasted_iota(jnp.int32, (ROWS, ROWS), 1)
        bias_p = jnp.where(has_left, 0.0, NEG)
        bias_b = jnp.where(jnp.logical_and(has_left, has_right), 0.0, NEG)
        k_c, k_p = kv_own[h, 0], kv_prv[h, 0]
        q_o, q_n = qdo_own[h, 0], qdo_nxt[h, 0]
        s_c = jnp.where(key_i <= query_i, nt(k_c, q_o) * SCALE2, NEG)
        s_p = nt(k_p, q_o) * SCALE2 + bias_p
        m_a = jnp.maximum(
            jnp.max(s_c, axis=0, keepdims=True), jnp.max(s_p, axis=0, keepdims=True)
        )
        p_c = jnp.exp2(s_c - m_a)
        p_p = jnp.exp2(s_p - m_a)
        l_a = jnp.sum(p_c, axis=0, keepdims=True) + jnp.sum(p_p, axis=0, keepdims=True)
        dp_c = nt(kv_own[h, 1], qdo_own[h, 1])
        dp_p = nt(kv_prv[h, 1], qdo_own[h, 1])
        d_a = jnp.sum(p_c * dp_c, axis=0, keepdims=True) + jnp.sum(
            p_p * dp_p, axis=0, keepdims=True
        )
        pbuf[slot, 0] = p_c
        pbuf[slot, 1] = p_p
        dpbuf[slot, 0] = dp_c
        dpbuf[slot, 1] = dp_p
        sa_own[h, 0:1] = m_a
        sa_own[h, 1:2] = l_a
        sa_own[h, 2:3] = d_a
        sa_own[h, 3:4] = d_a

        @pl.when(has_left)
        def _():
            c_sa(h).start()

        s_b = jnp.where(key_i > query_i, nt(k_p, q_n) * SCALE2 + bias_b, NEG)
        m_b = jnp.max(s_b, axis=0, keepdims=True)
        p_b = jnp.exp2(s_b - m_b)
        l_b = jnp.sum(p_b, axis=0, keepdims=True)
        dp_b = nt(kv_prv[h, 1], qdo_nxt[h, 1])
        d_b = jnp.sum(p_b * dp_b, axis=0, keepdims=True)
        pbuf[slot, 2] = p_b
        dpbuf[slot, 2] = dp_b
        sb_own[h, 0:1] = m_b
        sb_own[h, 1:2] = l_b
        sb_own[h, 2:3] = d_b
        sb_own[h, 3:4] = d_b

        @pl.when(has_right)
        def _():
            c_sb(h).start()

    def combine(a, b):
        m_a, m_b = a[0:1], b[0:1]
        m = jnp.maximum(m_a, m_b)
        e_a = jnp.exp2(m_a - m)
        e_b = jnp.exp2(m_b - m)
        inv = 1.0 / (a[1:2] * e_a + b[1:2] * e_b)
        w_a = e_a * inv
        w_b = e_b * inv
        return w_a, w_b, a[2:3] * w_a + b[2:3] * w_b

    def phase2(h):
        slot = lax.rem(h, SLOTS)

        @pl.when(has_left)
        def _():
            c_sb(h).wait_recv()

        @pl.when(has_right)
        def _():
            c_sa(h).wait_recv()

        w_o, _, delta_o = combine(sa_own[h], sb_rcv[h])
        _, w_n, delta_n = combine(sa_nxt[h], sb_own[h])
        k_c, k_p = kv_own[h, 0], kv_prv[h, 0]
        q_o, q_n = qdo_own[h, 0], qdo_nxt[h, 0]
        do_o, do_n = qdo_own[h, 1], qdo_nxt[h, 1]
        p_b = pbuf[slot, 2] * w_n
        ds_b = (p_b * (dpbuf[slot, 2] - delta_n)).astype(BF)
        p_p = pbuf[slot, 1] * w_o
        ds_p = (p_p * (dpbuf[slot, 1] - delta_o)).astype(BF)
        dkv_snd[h, 0] = ((nn(ds_p, q_o) + nn(ds_b, q_n)) * SCALE).astype(BF)
        dkv_snd[h, 1] = (nn(p_p.astype(BF), do_o) + nn(p_b.astype(BF), do_n)).astype(BF)

        @pl.when(has_left)
        def _():
            c_dkv(h).start()

        dq_snd[h] = (tn(ds_b, k_p) * SCALE).astype(BF)

        @pl.when(has_right)
        def _():
            c_dq(h).start()

        p_c = pbuf[slot, 0] * w_o
        ds_c = (p_c * (dpbuf[slot, 0] - delta_o)).astype(BF)
        dkv_loc[h, 0] = nn(ds_c, q_o) * SCALE
        dkv_loc[h, 1] = nn(p_c.astype(BF), do_o)
        dq_loc[h] = (tn(ds_c, k_c) + tn(ds_p, k_p)) * SCALE

    def out_byte(part, h):
        cb = part * HEADS + h
        return pltpu.make_async_copy(
            out_b.at[h, part], bg_ref.at[0, :, cols(cb)], ob_sem.at[h, part]
        )

    def out_patch(part, h):
        cb = part * HEADS + h
        return pltpu.make_async_copy(
            out_p.at[h, part], pg_ref.at[0, :, cols(cb)], op_sem.at[h, part]
        )

    def results(h):
        @pl.when(has_left)
        def _():
            c_dq(h).wait_recv()

        @pl.when(has_right)
        def _():
            c_dkv(h).wait_recv()

        for part in range(3):
            cb = part * HEADS + h
            if part == 0:
                grad = dq_loc[h] + dq_rcv[h].astype(F32)
            else:
                grad = dkv_loc[h, part - 1] + dkv_rcv[h, part - 1].astype(F32)
            high = grad.astype(BF)
            out_b[h, part] = high
            low = (grad - high.astype(F32)).astype(BF)
            sums = nn(mem[...], high) + nn(mem[...], low)
            ssum[h, part] = sums[:CAP]
            lead_sum = sums[CAP : CAP + 1]
            ls_snd[h, part : part + 1] = lead_sum
            if part == 0:
                ls_snd[h, 3:4] = lead_sum
            table = tab_v[:CAP, cols(cb)].astype(F32)
            g_acc[0, cb] = (
                jnp.sum(sums[:CAP] * table, axis=0, keepdims=True) + lead_sum * prev_rcv[cb]
            )
            out_byte(part, h).start()

        @pl.when(has_left)
        def _():
            c_ls(h).start()

    def patch_results(h):
        @pl.when(has_right)
        def _():
            c_ls(h).wait_recv()

        for part in range(3):
            cb = part * HEADS + h
            total = ssum[h, part] + last_col[...] * ls_rcv[h, part : part + 1]
            out_p[h, part] = (total * gain_ref[:, cols(cb)]).astype(BF)
            out_patch(part, h).start()

    def step(s, carry):
        @pl.when(s < HEADS)
        def _():
            phase1(s)

        @pl.when(s < HEADS - AHEAD)
        def _():
            send_inputs(s + AHEAD)

        @pl.when(jnp.logical_and(s >= LAG2, s < HEADS + LAG2))
        def _():
            phase2(s - LAG2)

        @pl.when(jnp.logical_and(s >= LAG3, s < HEADS + LAG3))
        def _():
            results(s - LAG3)

        @pl.when(jnp.logical_and(s >= LAG4, s < HEADS + LAG4))
        def _():
            patch_results(s - LAG4)

        return carry

    lax.fori_loop(0, HEADS + LAG4, step, 0)

    for t, group in enumerate(groups):
        copies = []
        for k, peer in enumerate(group):
            copy = pltpu.make_async_remote_copy(
                src_ref=g_acc.at[t],
                dst_ref=g_rcv.at[t, k],
                send_sem=gs_sem.at[t, k],
                recv_sem=gr_sem.at[t, k],
                device_id=peer,
                device_id_type=MESH,
            )
            copy.start()
            copies.append(copy)
        for copy in copies:
            copy.wait_recv()
        total = g_acc[t]
        for k in range(7):
            total = total + g_rcv[t, k]
        if t < 2:
            g_acc[t + 1] = total
        else:
            gg_ref[...] = total / ROWS
        for copy in copies:
            copy.wait_send()

    def drain(h, carry):
        @pl.when(has_left)
        def _():
            for copy in (c_q(h), c_do(h), c_sa(h), c_dkv(h), c_ls(h)):
                copy.wait_send()

        @pl.when(has_right)
        def _():
            for copy in (c_kv(h), c_sb(h), c_dq(h)):
                copy.wait_send()

        for part in range(3):
            out_byte(part, h).wait()
            out_patch(part, h).wait()
        return carry

    lax.fori_loop(0, HEADS, drain, 0)

    @pl.when(has_right)
    def _():
        c_prev.wait_send()


def local(byte_qkv, patch_qkv, patch_gain, out_grad, patch_slot, lead):
    width = 3 * HEADS * HD
    any_spec = pl.BlockSpec(memory_space=pl.ANY)
    vmem = pl.BlockSpec(memory_space=pltpu.VMEM)
    smem = pl.BlockSpec(memory_space=pltpu.SMEM)
    V = pltpu.VMEM
    byte_grad, patch_grad, gain_grad = pl.pallas_call(
        kernel,
        out_shape=(
            jax.ShapeDtypeStruct((1, ROWS, width), BF),
            jax.ShapeDtypeStruct((1, CAP, width), BF),
            jax.ShapeDtypeStruct((3 * HEADS, 1, HD), F32),
        ),
        in_specs=[any_spec, any_spec, vmem, any_spec, vmem, smem],
        out_specs=(any_spec, any_spec, vmem),
        scratch_shapes=[
            V((ROWS, width), BF),
            V((HD, width), BF),
            V((ROWS, HD), BF),
            V((80, ROWS), BF),
            V((HEADS, 2, ROWS, HD), BF),
            V((HEADS, 2, ROWS, HD), BF),
            V((HEADS, 2, ROWS, HD), BF),
            V((HEADS, 2, ROWS, HD), BF),
            V((HEADS, ROWS, HD), F32),
            V((HEADS, 2, ROWS, HD), F32),
            V((HEADS, ROWS, HD), BF),
            V((HEADS, 2, ROWS, HD), BF),
            V((HEADS, ROWS, HD), BF),
            V((HEADS, 2, ROWS, HD), BF),
            V((SLOTS, 3, ROWS, ROWS), F32),
            V((SLOTS, 3, ROWS, ROWS), F32),
            V((HEADS, 4, ROWS), F32),
            V((HEADS, 4, ROWS), F32),
            V((HEADS, 4, ROWS), F32),
            V((HEADS, 4, ROWS), F32),
            V((3 * HEADS, 1, HD), F32),
            V((3 * HEADS, 1, HD), F32),
            V((HEADS, 4, HD), F32),
            V((HEADS, 4, HD), F32),
            V((CAP, HD), F32),
            V((HEADS, 3, CAP, HD), F32),
            V((HEADS, 3, ROWS, HD), BF),
            V((HEADS, 3, CAP, HD), BF),
            V((3, 3 * HEADS, 1, HD), F32),
            V((3, 7, 3 * HEADS, 1, HD), F32),
            pltpu.SemaphoreType.DMA((2,)),
            pltpu.SemaphoreType.DMA((HEADS,)),
            pltpu.SemaphoreType.DMA((8, HEADS)),
            pltpu.SemaphoreType.DMA((8, HEADS)),
            pltpu.SemaphoreType.DMA((2,)),
            pltpu.SemaphoreType.DMA((HEADS, 3)),
            pltpu.SemaphoreType.DMA((HEADS, 3)),
            pltpu.SemaphoreType.DMA((3, 7)),
            pltpu.SemaphoreType.DMA((3, 7)),
        ],
        compiler_params=pltpu.CompilerParams(
            collective_id=0, has_side_effects=True, vmem_limit_bytes=48 * 2**20
        ),
    )(byte_qkv, patch_qkv, patch_gain.reshape(1, width), out_grad, patch_slot, lead)
    return byte_grad, patch_grad, gain_grad.reshape(width)


def solution(mesh):
    placed = (
        P("dp", "seq", None),
        P("dp", "seq", None),
        P(),
        P("dp", "seq", None),
        P("dp", "seq"),
        P("dp", "seq"),
    )
    return jax.shard_map(
        local,
        mesh=mesh,
        in_specs=placed,
        out_specs=(P("dp", "seq", None), P("dp", "seq", None), P()),
        check_vma=False,
    )
```

time: 349 us -> 95.1 us (0.27)
  waiting for transfers between devices: 157 us -> 0 us
  blocking collectives: 137 us -> 0 us
  Pallas kernels: 0 us -> 86.2 us
  matrix products: 23.3 us -> 0 us
  starting transfers between devices: 17.6 us -> 0 us
  other arithmetic: 9.05 us -> 0 us
  local copies, waits for them, and re-layouts: 1.51 us -> 7.31 us
    ppermute x6 -> x0, waiting for transfers between devices: 157 us -> none  [shifted(): lax.ppermute(value, axis, [(source, source + steps) for source in range(i...]
    psum x1 -> x0, blocking collectives: 137 us -> none  [local(): gain_grad = lax.psum(gain_term, ('seq', 'dp')) / row_count]
    pallas_call x0 -> x1, Pallas kernels: none -> 86.2 us  [local(): pl.pallas_call(kernel, out_shape=(jax.ShapeDtypeStruct((1, ROWS, width),...]
    dot_general x42 -> x0, matrix products: 23.3 us -> none  [the longest x8 5.63 us: local(): jnp.einsum('qe,ke->qk', cot_head, value_head, preferred_element_type=jnp....]
    ppermute x6 -> x0, starting transfers between devices: 17.6 us -> none  [shifted(): lax.ppermute(value, axis, [(source, source + steps) for source in range(i...]
    unnamed x18 -> x13, local copies, waits for them, and re-layouts: 0.12 us -> 7.31 us
  transfers between devices with their start and end apart: 6 -> 0, of which waited for: 6 -> 0; matrix products, arithmetic and copies ran while one was open for 1% -> 0% of each run, Pallas kernels for 0% -> 0%
where the time goes in v1:
time: 95.1 us; the launch traced here: 94.8 us
  Pallas kernels  86.2 us (91%)
  local copies, waits for them, and re-layouts  7.31 us (8%)
  between operations  1.3 us (1%)
    pallas_call x1, Pallas kernels, local(): pl.pallas_call(kernel, out_shape=(jax.ShapeDtypeStruct((1, ROWS, width),...  86.2 us
    unnamed x13, local copies, waits for them, and re-layouts  7.31 us

profile of v1, /device:TPU:1, one launch (start us, length us, event | category | flops | bytes accessed | tf_op | source)
XLA Modules:
  0.0 94.8 jit_solution(17993191177639727545)
XLA Ops:
  1.3 0.0 copy-start
  1.3 1.4 %copy-done = bf16[1,256,3072]{2,1,0:T(8,128)(2,1)S(1)} copy-done((bf16[1,256,3072]{2,1,0:T(8,128)(2,1)S(1)}, bf16[1,256,3072]{2,1,0:T(8,128)(2,1)}, u32[]{:S(2)}) %copy-start) | copy-done | bytes 1572888
  2.7 0.0 copy-start.1
  2.7 1.0 %copy-done.1 = bf16[1,256,1024]{2,1,0:T(8,128)(2,1)S(1)} copy-done((bf16[1,256,1024]{2,1,0:T(8,128)(2,1)S(1)}, bf16[1,256,1024]{2,1,0:T(8,128)(2,1)}, u32[]{:S(2)}) %copy-start.1) | copy-done | bytes 524312
  3.7 0.0 copy-start.2
  3.7 1.0 %copy-done.2 = bf16[1,64,3072]{2,1,0:T(8,128)(2,1)S(1)} copy-done((bf16[1,64,3072]{2,1,0:T(8,128)(2,1)S(1)}, bf16[1,64,3072]{2,1,0:T(8,128)(2,1)}, u32[]{:S(2)}) %copy-start.2) | copy-done | bytes 393240
  4.7 0.0 copy-start.3
  4.7 0.7 copy-done.3
  5.4 0.0 copy-start.4
  5.4 0.7 copy-done.4
  6.1 86.2 %shard_map.85 = (bf16[1,256,3072]{2,1,0:T(8,128)(2,1)S(1)}, bf16[1,64,3072]{2,1,0:T(8,128)(2,1)S(1)}, f32[24,1,128]{2,1,0:T(1,128)S(1)}) custom-call(bf16[1,256,3072]{2,1,0:T(8,128)(2,1)S(1)} %copy-done, bf16[1,64,3072]{2,1,0:T(8,128)(2,1)S(1)} %copy-done.2, f32[1,3072]{1,0:T(1,128)S(1)} %bitcast.2, bf16[1,256,1024]{2,1,0:T(8,128)(2,1)S(1)} %copy-done.1, ...), custom_call_target="tpu_custom_call" | custom-call | tf_op jit(solution)/shard_map/pallas_call | solution.py:518
  92.3 1.1 %copy.13 = bf16[1,256,3072]{2,1,0:T(8,128)(2,1)} copy(bf16[1,256,3072]{2,1,0:T(8,128)(2,1)S(1)} %get-tuple-element.12) | data formatting | bytes 3145728
  93.4 0.7 copy.14
  94.2 0.6 copy.15
Async XLA Ops:
  1.3 1.4 %copy-start = (bf16[1,256,3072]{2,1,0:T(8,128)(2,1)S(1)}, bf16[1,256,3072]{2,1,0:T(8,128)(2,1)}, u32[]{:S(2)}) copy-start(bf16[1,256,3072]{2,1,0:T(8,128)(2,1)} %byte_ref.1) | copy-start | bytes 4718596
  2.7 1.0 %copy-start.1 = (bf16[1,256,1024]{2,1,0:T(8,128)(2,1)S(1)}, bf16[1,256,1024]{2,1,0:T(8,128)(2,1)}, u32[]{:S(2)}) copy-start(bf16[1,256,1024]{2,1,0:T(8,128)(2,1)} %cot_ref.1) | copy-start | bytes 1572868
  3.7 1.0 %copy-start.2 = (bf16[1,64,3072]{2,1,0:T(8,128)(2,1)S(1)}, bf16[1,64,3072]{2,1,0:T(8,128)(2,1)}, u32[]{:S(2)}) copy-start(bf16[1,64,3072]{2,1,0:T(8,128)(2,1)} %patch_ref.1) | copy-start | bytes 1179652
  4.7 0.7 copy-start.3
  5.4 0.7 copy-start.4

commit v2 on v1

--- a/solution.py
+++ b/solution.py
@@ -22,11 +22,14 @@
 SCALE2 = SCALE / math.log(2.0)
 AHEAD = 3
 LAG2 = 3
-LAG3 = 5
-LAG4 = 6
+EXT = 80
 SLOTS = LAG2 + 1
-
-K_Q, K_DO, K_KV, K_SA, K_SB, K_DKV, K_DQ, K_LS = range(8)
+FLIGHT = 3
+HOLD = 6
+FIRST = 7
+
+K_Q, K_DO, K_KV, K_SA, K_SB, K_DKV, K_DQ, K_TQ, K_TX = range(9)
+O_PREV, O_EL, O_ER, O_LP, O_LS = range(5)
 
 
 def nt(a, b):
@@ -58,7 +61,7 @@
         p = lax.rem(x * 2 + core + k, 8)
         along_xc.append(((z_lo * 4 + p // 2) * 8 + y, z_hi * 2 + lax.rem(p, 2)))
         along_y.append(((z_lo * 4 + x) * 8 + lax.rem(y + k, 8), dp))
-    return along_z, along_xc, along_y
+    return along_y, along_z, along_xc
 
 
 def kernel(
@@ -72,9 +75,17 @@
     pg_ref,
     gg_ref,
     byte_v,
-    tab_v,
+    tabq,
+    tabx,
+    tabq_rcv,
+    tabx_rcv,
     oh,
     mem,
+    mem_l,
+    mem_r,
+    effs,
+    effs_l,
+    effs_r,
     qdo_own,
     kv_own,
     qdo_nxt,
@@ -93,8 +104,11 @@
     sb_rcv,
     prev_snd,
     prev_rcv,
+    lp_snd,
+    lp_rcv,
     ls_snd,
     ls_rcv,
+    from_q,
     last_col,
     ssum,
     out_b,
@@ -103,9 +117,12 @@
     g_rcv,
     in_sem,
     do_sem,
+    tab_sem,
     s_sem,
     r_sem,
-    prev_sem,
+    one_s,
+    one_r,
+    hi_sem,
     ob_sem,
     op_sem,
     gs_sem,
@@ -129,13 +146,37 @@
     def _():
         pl.semaphore_signal(barrier, inc=1, device_id=right, device_id_type=MESH)
 
-    for group in groups:
-        for peer in group:
+    z_lo = me // 32
+    z_hi = dp // 2
+    place = lax.rem(me, 32)
+    other_half = [(k * 32 + place, (1 - z_hi) * 2 + lax.rem(dp, 2)) for k in range(4)]
+    same_half = [(lax.rem(z_lo + k, 4) * 32 + place, dp) for k in range(1, 4)]
+    for peer in groups[0] + groups[2] + same_half:
+        pl.semaphore_signal(barrier, inc=1, device_id=peer, device_id_type=MESH)
+
+    @pl.when(z_hi == 0)
+    def _():
+        for peer in other_half:
             pl.semaphore_signal(barrier, inc=1, device_id=peer, device_id_type=MESH)
 
-    load_tab = pltpu.make_async_copy(patch_ref.at[0], tab_v.at[pl.ds(0, CAP)], in_sem.at[0])
-    load_tab.start()
-    load_byte = pltpu.make_async_copy(byte_ref.at[0], byte_v, in_sem.at[1])
+    def load_tables(h):
+        return [
+            pltpu.make_async_copy(
+                patch_ref.at[0, :, cols(h)], tabq.at[h], tab_sem.at[h, 0]
+            )
+        ] + [
+            pltpu.make_async_copy(
+                patch_ref.at[0, :, cols((part + 1) * HEADS + h)],
+                tabx.at[h, part, pl.ds(0, CAP)],
+                tab_sem.at[h, part + 1],
+            )
+            for part in range(2)
+        ]
+
+    for h in range(HEADS):
+        for load in load_tables(h):
+            load.start()
+    load_byte = pltpu.make_async_copy(byte_ref.at[0], byte_v, in_sem.at[0])
     load_byte.start()
 
     def load_do(h):
@@ -146,17 +187,24 @@
 
     lead = lead_ref[0, 0]
     slots = slot_ref[...]
-    row_i = lax.broadcasted_iota(jnp.int32, (HD, ROWS), 0)
-    lane_i = lax.broadcasted_iota(jnp.int32, (HD, ROWS), 1)
-    pick = jnp.where(row_i == slots, 1.0, 0.0)
-    oh[...] = jnp.transpose(pick).astype(BF)
-    mem[...] = jnp.where(lane_i < lead, jnp.where(row_i == CAP, 1.0, 0.0), pick)[:80].astype(BF)
+    lane_i = lax.broadcasted_iota(jnp.int32, (1, ROWS), 1)
+    effs[...] = jnp.where(lane_i < lead, CAP, slots).astype(F32)
+
+    def members(eff):
+        row_i = lax.broadcasted_iota(jnp.int32, (EXT, ROWS), 0).astype(F32)
+        return jnp.where(row_i == eff, 1.0, 0.0).astype(BF)
+
+    mem[...] = members(effs[...])
+    slot_i = lax.broadcasted_iota(jnp.int32, (HD, ROWS), 0)
+    pick = jnp.where(slot_i == slots, 1.0, 0.0)
+    oh[...] = jnp.transpose(pick)[:, :CAP].astype(BF)
     last_col[...] = jnp.broadcast_to(pick[:CAP, ROWS - 1 : ROWS], (CAP, HD))
-    tab_v[CAP:] = jnp.zeros((HD - CAP, 3 * HEADS * HD), BF)
 
     @pl.when(jnp.logical_not(has_left))
     def _():
         kv_prv[...] = jnp.zeros_like(kv_prv)
+        tabx_rcv[...] = jnp.zeros_like(tabx_rcv)
+        effs_l[...] = jnp.zeros_like(effs_l)
         dq_rcv[...] = jnp.zeros_like(dq_rcv)
         prev_rcv[...] = jnp.zeros_like(prev_rcv)
         sb_rcv[...] = jnp.full(sb_rcv.shape, NEG, F32)
@@ -166,9 +214,14 @@
         qdo_nxt[...] = jnp.zeros_like(qdo_nxt)
         dkv_rcv[...] = jnp.zeros_like(dkv_rcv)
         ls_rcv[...] = jnp.zeros_like(ls_rcv)
+        lp_rcv[...] = jnp.zeros_like(lp_rcv)
+        tabq_rcv[...] = jnp.zeros_like(tabq_rcv)
+        effs_r[...] = jnp.zeros_like(effs_r)
         sa_nxt[...] = jnp.ones_like(sa_nxt)
 
-    load_tab.wait()
+    for h in range(HEADS):
+        for load in load_tables(h):
+            load.wait()
     load_byte.wait()
 
     def hidden_dst(part, h):
@@ -177,7 +230,7 @@
     def make_hidden(h, carry):
         for part in range(3):
             cb = part * HEADS + h
-            rows = nn(oh[...], tab_v[:, cols(cb)])
+            rows = nn(oh[...], tabq[h] if part == 0 else tabx[h, part - 1, :CAP])
             prev_snd[cb] = rows[ROWS - 1 : ROWS]
             hidden = gain_ref[:, cols(cb)] * rows + byte_v[:, cols(cb)].astype(F32)
             hidden_dst(part, h)[...] = hidden.astype(BF)
@@ -188,7 +241,13 @@
         load_do(h).wait()
 
     neighbours = has_left.astype(jnp.int32) + has_right.astype(jnp.int32)
-    pl.semaphore_wait(barrier, neighbours + 21)
+    pl.semaphore_wait(barrier, neighbours + 17 + 4 * z_hi)
+
+    @pl.when(z_hi == 1)
+    def _():
+        for peer in other_half:
+            pl.semaphore_signal(hi_sem, inc=1, device_id=peer, device_id_type=MESH)
+
 
     def remote(kind, h, src, dst, to):
         return pltpu.make_async_remote_copy(
@@ -221,33 +280,49 @@
     def c_dq(h):
         return remote(K_DQ, h, dq_snd.at[h], dq_rcv.at[h], right)
 
-    def c_ls(h):
-        return remote(K_LS, h, ls_snd.at[h], ls_rcv.at[h], left)
-
-    c_prev = pltpu.make_async_remote_copy(
-        src_ref=prev_snd,
-        dst_ref=prev_rcv,
-        send_sem=prev_sem.at[0],
-        recv_sem=prev_sem.at[1],
-        device_id=right,
-        device_id_type=MESH,
-    )
+    def c_tq(h):
+        return remote(K_TQ, h, tabq.at[h], tabq_rcv.at[h], left)
+
+    def c_tx(h):
+        return remote(K_TX, h, tabx.at[h], tabx_rcv.at[h], right)
+
+    def once(kind, src, dst, to):
+        return pltpu.make_async_remote_copy(
+            src_ref=src,
+            dst_ref=dst,
+            send_sem=one_s.at[kind],
+            recv_sem=one_r.at[kind],
+            device_id=to,
+            device_id_type=MESH,
+        )
+
+    c_prev = once(O_PREV, prev_snd, prev_rcv, right)
+    c_el = once(O_EL, effs, effs_r, left)
+    c_er = once(O_ER, effs, effs_l, right)
+    c_lp = once(O_LP, lp_snd, lp_rcv, left)
+    c_ls = once(O_LS, ls_snd, ls_rcv, left)
 
     @pl.when(has_right)
     def _():
         c_prev.start()
+        c_er.start()
 
     @pl.when(has_left)
     def _():
+        c_el.start()
         for h in range(AHEAD):
             c_do(h).start()
         c_prev.wait_recv()
 
     lead_rows = lax.broadcasted_iota(jnp.int32, (16, HD), 0) < lead
 
+    first_row = lax.broadcasted_iota(jnp.int32, (EXT - CAP, HD), 0) == 0
+
     def fix_hidden(h, carry):
         for part in range(3):
             cb = part * HEADS + h
+            if part > 0:
+                tabx[h, part - 1, CAP:] = jnp.where(first_row, prev_rcv[cb], 0.0).astype(BF)
             dst = hidden_dst(part, h)
             fixed = gain_ref[:, cols(cb)] * prev_rcv[cb] + byte_v[:16, cols(cb)].astype(F32)
             dst[:16] = jnp.where(lead_rows, fixed, dst[:16].astype(F32)).astype(BF)
@@ -268,6 +343,17 @@
 
     for h in range(AHEAD):
         send_inputs(h, False)
+
+    @pl.when(has_left)
+    def _():
+        c_er.wait_recv()
+
+    @pl.when(has_right)
+    def _():
+        c_el.wait_recv()
+
+    mem_l[...] = members(effs_l[...])
+    mem_r[...] = members(effs_r[...])
 
     def phase1(h):
         slot = lax.rem(h, SLOTS)
@@ -360,24 +446,60 @@
         ds_b = (p_b * (dpbuf[slot, 2] - delta_n)).astype(BF)
         p_p = pbuf[slot, 1] * w_o
         ds_p = (p_p * (dpbuf[slot, 1] - delta_o)).astype(BF)
-        dkv_snd[h, 0] = ((nn(ds_p, q_o) + nn(ds_b, q_n)) * SCALE).astype(BF)
-        dkv_snd[h, 1] = (nn(p_p.astype(BF), do_o) + nn(p_b.astype(BF), do_n)).astype(BF)
-
-        @pl.when(has_left)
-        def _():
-            c_dkv(h).start()
-
-        dq_snd[h] = (tn(ds_b, k_p) * SCALE).astype(BF)
-
-        @pl.when(has_right)
-        def _():
-            c_dq(h).start()
+        dq_n = (tn(ds_b, k_p) * SCALE).astype(BF)
+        dq_snd[h] = dq_n
+        dk_p = ((nn(ds_p, q_o) + nn(ds_b, q_n)) * SCALE).astype(BF)
+        dv_p = (nn(p_p.astype(BF), do_o) + nn(p_b.astype(BF), do_n)).astype(BF)
+        dkv_snd[h, 0] = dk_p
+        dkv_snd[h, 1] = dv_p
 
         p_c = pbuf[slot, 0] * w_o
         ds_c = (p_c * (dpbuf[slot, 0] - delta_o)).astype(BF)
-        dkv_loc[h, 0] = nn(ds_c, q_o) * SCALE
-        dkv_loc[h, 1] = nn(p_c.astype(BF), do_o)
-        dq_loc[h] = (tn(ds_c, k_c) + tn(ds_p, k_p)) * SCALE
+        dk = nn(ds_c, q_o) * SCALE
+        dv = nn(p_c.astype(BF), do_o)
+        dq = (tn(ds_c, k_c) + tn(ds_p, k_p)) * SCALE
+        dkv_loc[h, 0] = dk
+        dkv_loc[h, 1] = dv
+        dq_loc[h] = dq
+
+    def phase3(h):
+        @pl.when(has_left)
+        def _():
+            c_tx(h).wait_recv()
+
+        @pl.when(has_right)
+        def _():
+            c_tq(h).wait_recv()
+
+        def own_sums(grad):
+            high = grad.astype(BF)
+            low = (grad - high.astype(F32)).astype(BF)
+            return nn(mem[...], high) + nn(mem[...], low)
+
+        def column_sum(x):
+            return jnp.sum(x, axis=0, keepdims=True)
+
+        sums = own_sums(dq_loc[h])
+        ssum[h, 0] = sums[:CAP]
+        ls_snd[h, 0:1] = sums[CAP : CAP + 1]
+        sent = nn(mem_r[...], dq_snd[h])
+        from_q[h, 0:1] = sent[CAP : CAP + 1]
+        g_acc[0, h] = (
+            column_sum(sums[:CAP] * tabq[h].astype(F32))
+            + sums[CAP : CAP + 1] * prev_rcv[h]
+            + column_sum(sent[:CAP] * tabq_rcv[h].astype(F32))
+            + sent[CAP : CAP + 1] * prev_snd[h]
+        )
+        for part in range(2):
+            sums = own_sums(dkv_loc[h, part])
+            ssum[h, part + 1] = sums[:CAP]
+            ls_snd[h, part + 1 : part + 2] = sums[CAP : CAP + 1]
+            sent = nn(mem_l[...], dkv_snd[h, part])
+            lp_snd[h, part : part + 1] = sent[CAP : CAP + 1]
+            g_acc[0, (part + 1) * HEADS + h] = column_sum(
+                sums * tabx[h, part].astype(F32)
+            ) + column_sum(sent * tabx_rcv[h, part].astype(F32))
+        ls_snd[h, 3:4] = sums[CAP : CAP + 1]
 
     def out_byte(part, h):
         cb = part * HEADS + h
@@ -391,6 +513,27 @@
             out_p.at[h, part], pg_ref.at[0, :, cols(cb)], op_sem.at[h, part]
         )
 
+    def send_dkv(h):
+        @pl.when(has_left)
+        def _():
+            c_dkv(h).start()
+
+    def send_dq(h):
+        @pl.when(has_right)
+        def _():
+            c_dq(h).start()
+
+    def send_tables():
+        @pl.when(has_left)
+        def _():
+            for h in range(HEADS):
+                c_tq(h).start()
+
+        @pl.when(has_right)
+        def _():
+            for h in range(HEADS):
+                c_tx(h).start()
+
     def results(h):
         @pl.when(has_left)
         def _():
@@ -400,39 +543,22 @@
         def _():
             c_dkv(h).wait_recv()
 
+        for part in range(3):
+            if part == 0:
+                own, got = dq_loc[h], dq_rcv[h]
+            else:
+                own, got = dkv_loc[h, part - 1], dkv_rcv[h, part - 1]
+            out_b[h, part] = (own + got.astype(F32)).astype(BF)
+            out_byte(part, h).start()
+            ssum[h, part] += nn(mem[:CAP], got)
+
+    def patch_results(h):
         for part in range(3):
             cb = part * HEADS + h
+            after = ls_rcv[h, part : part + 1]
             if part == 0:
-                grad = dq_loc[h] + dq_rcv[h].astype(F32)
-            else:
-                grad = dkv_loc[h, part - 1] + dkv_rcv[h, part - 1].astype(F32)
-            high = grad.astype(BF)
-            out_b[h, part] = high
-            low = (grad - high.astype(F32)).astype(BF)
-            sums = nn(mem[...], high) + nn(mem[...], low)
-            ssum[h, part] = sums[:CAP]
-            lead_sum = sums[CAP : CAP + 1]
-            ls_snd[h, part : part + 1] = lead_sum
-            if part == 0:
-                ls_snd[h, 3:4] = lead_sum
-            table = tab_v[:CAP, cols(cb)].astype(F32)
-            g_acc[0, cb] = (
-                jnp.sum(sums[:CAP] * table, axis=0, keepdims=True) + lead_sum * prev_rcv[cb]
-            )
-            out_byte(part, h).start()
-
-        @pl.when(has_left)
-        def _():
-            c_ls(h).start()
-
-    def patch_results(h):
-        @pl.when(has_right)
-        def _():
-            c_ls(h).wait_recv()
-
-        for part in range(3):
-            cb = part * HEADS + h
-            total = ssum[h, part] + last_col[...] * ls_rcv[h, part : part + 1]
+                after = after + from_q[h, 0:1]
+            total = ssum[h, part] + last_col[...] * after
             out_p[h, part] = (total * gain_ref[:, cols(cb)]).astype(BF)
             out_patch(part, h).start()
 
@@ -445,26 +571,29 @@
         def _():
             send_inputs(s + AHEAD)
 
-        @pl.when(jnp.logical_and(s >= LAG2, s < HEADS + LAG2))
+        @pl.when(s == HEADS - AHEAD)
+        def _():
+            send_tables()
+
+        @pl.when(s >= LAG2)
         def _():
             phase2(s - LAG2)
 
-        @pl.when(jnp.logical_and(s >= LAG3, s < HEADS + LAG3))
-        def _():
-            results(s - LAG3)
-
-        @pl.when(jnp.logical_and(s >= LAG4, s < HEADS + LAG4))
-        def _():
-            patch_results(s - LAG4)
+        @pl.when(jnp.logical_and(s >= FIRST, s < FIRST + FLIGHT))
+        def _():
+            send_dkv(s - FIRST)
+
+        @pl.when(s >= FIRST)
+        def _():
+            send_dq(s - FIRST)
 
         return carry
 
-    lax.fori_loop(0, HEADS + LAG4, step, 0)
-
-    for t, group in enumerate(groups):
-        copies = []
-        for k, peer in enumerate(group):
-            copy = pltpu.make_async_remote_copy(
+    lax.fori_loop(0, HEADS + LAG2, step, 0)
+
+    def gain_copies(t):
+        return [
+            pltpu.make_async_remote_copy(
                 src_ref=g_acc.at[t],
                 dst_ref=g_rcv.at[t, k],
                 send_sem=gs_sem.at[t, k],
@@ -472,9 +601,15 @@
                 device_id=peer,
                 device_id_type=MESH,
             )
+            for k, peer in enumerate(groups[t])
+        ]
+
+    def gain_start(t):
+        for copy in gain_copies(t):
             copy.start()
-            copies.append(copy)
-        for copy in copies:
+
+    def gain_finish(t):
+        for copy in gain_copies(t):
             copy.wait_recv()
         total = g_acc[t]
         for k in range(7):
@@ -483,18 +618,80 @@
             g_acc[t + 1] = total
         else:
             gg_ref[...] = total / ROWS
-        for copy in copies:
+
+    def run_phase3(h, carry):
+        phase3(h)
+        return carry
+
+    lax.fori_loop(0, HEADS, run_phase3, 0)
+    gain_start(0)
+
+    @pl.when(has_left)
+    def _():
+        c_lp.start()
+
+    for h in range(FLIGHT, HOLD):
+        send_dkv(h)
+    for h in range(HEADS + LAG2 - FIRST, HEADS):
+        send_dq(h)
+
+    def add_lead(h, carry):
+        ls_snd[h, 1:3] = ls_snd[h, 1:3] + lp_rcv[h]
+        return carry
+
+    def forward_lead():
+        @pl.when(has_right)
+        def _():
+            c_lp.wait_recv()
+
+        lax.fori_loop(0, HEADS, add_lead, 0)
+
+        @pl.when(has_left)
+        def _():
+            c_ls.start()
+
+    def take_lead():
+        @pl.when(has_right)
+        def _():
+            c_ls.wait_recv()
+
+    for h in range(HEADS):
+        results(h)
+        if h == 1:
+            forward_lead()
+            for g in range(HOLD, HEADS):
+                send_dkv(g)
+        if h == 2:
+            gain_finish(0)
+
+            @pl.when(z_hi == 0)
+            def _():
+                pl.semaphore_wait(hi_sem, 4)
+
+            gain_start(1)
+        if h == 4:
+            gain_finish(1)
+            gain_start(2)
+        if h == 6:
+            take_lead()
+            for g in range(6):
+                patch_results(g)
+            gain_finish(2)
+        if h >= 6:
+            patch_results(h)
+    for t in range(3):
+        for copy in gain_copies(t):
             copy.wait_send()
 
     def drain(h, carry):
         @pl.when(has_left)
         def _():
-            for copy in (c_q(h), c_do(h), c_sa(h), c_dkv(h), c_ls(h)):
+            for copy in (c_q(h), c_do(h), c_tq(h), c_sa(h), c_dkv(h)):
                 copy.wait_send()
 
         @pl.when(has_right)
         def _():
-            for copy in (c_kv(h), c_sb(h), c_dq(h)):
+            for copy in (c_kv(h), c_tx(h), c_sb(h), c_dq(h)):
                 copy.wait_send()
 
         for part in range(3):
@@ -504,9 +701,15 @@
 
     lax.fori_loop(0, HEADS, drain, 0)
 
+    @pl.when(has_left)
+    def _():
+        for copy in (c_el, c_lp, c_ls):
+            copy.wait_send()
+
     @pl.when(has_right)
     def _():
-        c_prev.wait_send()
+        for copy in (c_prev, c_er):
+            copy.wait_send()
 
 
 def local(byte_qkv, patch_qkv, patch_gain, out_grad, patch_slot, lead):
@@ -526,9 +729,17 @@
         out_specs=(any_spec, any_spec, vmem),
         scratch_shapes=[
             V((ROWS, width), BF),
-            V((HD, width), BF),
-            V((ROWS, HD), BF),
-            V((80, ROWS), BF),
+            V((HEADS, CAP, HD), BF),
+            V((HEADS, 2, EXT, HD), BF),
+            V((HEADS, CAP, HD), BF),
+            V((HEADS, 2, EXT, HD), BF),
+            V((ROWS, CAP), BF),
+            V((EXT, ROWS), BF),
+            V((EXT, ROWS), BF),
+            V((EXT, ROWS), BF),
+            V((1, ROWS), F32),
+            V((1, ROWS), F32),
+            V((1, ROWS), F32),
             V((HEADS, 2, ROWS, HD), BF),
             V((HEADS, 2, ROWS, HD), BF),
             V((HEADS, 2, ROWS, HD), BF),
@@ -547,26 +758,32 @@
             V((HEADS, 4, ROWS), F32),
             V((3 * HEADS, 1, HD), F32),
             V((3 * HEADS, 1, HD), F32),
+            V((HEADS, 2, HD), F32),
+            V((HEADS, 2, HD), F32),
             V((HEADS, 4, HD), F32),
             V((HEADS, 4, HD), F32),
+            V((HEADS, 1, HD), F32),
             V((CAP, HD), F32),
             V((HEADS, 3, CAP, HD), F32),
             V((HEADS, 3, ROWS, HD), BF),
             V((HEADS, 3, CAP, HD), BF),
             V((3, 3 * HEADS, 1, HD), F32),
             V((3, 7, 3 * HEADS, 1, HD), F32),
-            pltpu.SemaphoreType.DMA((2,)),
+            pltpu.SemaphoreType.DMA((1,)),
             pltpu.SemaphoreType.DMA((HEADS,)),
-            pltpu.SemaphoreType.DMA((8, HEADS)),
-            pltpu.SemaphoreType.DMA((8, HEADS)),
-            pltpu.SemaphoreType.DMA((2,)),
+            pltpu.SemaphoreType.DMA((HEADS, 3)),
+            pltpu.SemaphoreType.DMA((9, HEADS)),
+            pltpu.SemaphoreType.DMA((9, HEADS)),
+            pltpu.SemaphoreType.DMA((5,)),
+            pltpu.SemaphoreType.DMA((5,)),
+            pltpu.SemaphoreType.REGULAR,
             pltpu.SemaphoreType.DMA((HEADS, 3)),
             pltpu.SemaphoreType.DMA((HEADS, 3)),
             pltpu.SemaphoreType.DMA((3, 7)),
             pltpu.SemaphoreType.DMA((3, 7)),
         ],
         compiler_params=pltpu.CompilerParams(
-            collective_id=0, has_side_effects=True, vmem_limit_bytes=48 * 2**20
+            collective_id=0, has_side_effects=True, vmem_limit_bytes=62 * 2**20
         ),
     )(byte_qkv, patch_qkv, patch_gain.reshape(1, width), out_grad, patch_slot, lead)
     return byte_grad, patch_grad, gain_grad.reshape(width)

time: 95.1 us -> 82.8 us (0.87)
  the two profiles are of different devices: /device:TPU:1 before, /device:TPU:125 now
where the time goes in v2:
time: 82.8 us; the launch traced here: 82.5 us
  Pallas kernels  77.2 us (93%)
  local copies, waits for them, and re-layouts  4.05 us (5%)
  between operations  1.3 us (2%)
    pallas_call x1, Pallas kernels, local(): pl.pallas_call(kernel, out_shape=(jax.ShapeDtypeStruct((1, ROWS, width),...  77.2 us
    unnamed x7, local copies, waits for them, and re-layouts  4.05 us

profile of v2, /device:TPU:125, one launch (start us, length us, event | category | flops | bytes accessed | tf_op | source)
XLA Modules:
  0.0 82.5 jit_solution(430019470179496989)
XLA Ops:
  1.3 77.2 %shard_map.85 = (bf16[1,256,3072]{2,1,0:T(8,128)(2,1)}, bf16[1,64,3072]{2,1,0:T(8,128)(2,1)}, f32[24,1,128]{2,1,0:T(1,128)}) custom-call(bf16[1,256,3072]{2,1,0:T(8,128)(2,1)} %byte_ref.1, bf16[1,64,3072]{2,1,0:T(8,128)(2,1)} %patch_ref.1, f32[1,3072]{1,0:T(1,128)} %bitcast.2, bf16[1,256,1024]{2,1,0:T(8,128)(2,1)} %cot_ref.1, s32[1,256]{1,0:T(1,128)} %slot_ref.1, ...), custom_call_target="tpu_custom_call" | custom-call | tf_op jit(solution)/shard_map/pallas_call | solution.py:721
  78.4 0.0 copy-start
  78.5 0.0 copy-start.1
  78.5 2.7 %copy.13 = bf16[1,256,3072]{2,1,0:T(8,128)(2,1)} copy(bf16[1,256,3072]{2,1,0:T(8,128)(2,1)} %get-tuple-element.12) | data formatting | bytes 3145728
  81.2 0.0 copy-done
  81.2 0.7 copy.14
  81.9 0.0 copy-done.1
  81.9 0.6 copy.15
Async XLA Ops:
  78.4 2.7 %copy-start = (bf16[1,64,3072]{2,1,0:T(8,128)(2,1)S(1)}, bf16[1,64,3072]{2,1,0:T(8,128)(2,1)}, u32[]{:S(2)}) copy-start(bf16[1,64,3072]{2,1,0:T(8,128)(2,1)} %get-tuple-element.13) | copy-start | bytes 1179652
  78.5 3.5 %copy-start.1 = (f32[24,1,128]{2,1,0:T(1,128)S(1)}, f32[24,1,128]{2,1,0:T(1,128)}, u32[]{:S(2)}) copy-start(f32[24,1,128]{2,1,0:T(1,128)} %get-tuple-element.8) | copy-start | bytes 36868

commit v3 on v2

--- a/solution.py
+++ b/solution.py
@@ -24,12 +24,11 @@
 LAG2 = 3
 EXT = 80
 SLOTS = LAG2 + 1
-FLIGHT = 3
-HOLD = 6
+SENT = 3
 FIRST = 7
 
 K_Q, K_DO, K_KV, K_SA, K_SB, K_DKV, K_DQ, K_TQ, K_TX = range(9)
-O_PREV, O_EL, O_ER, O_LP, O_LS = range(5)
+O_PREV, O_EL, O_ER, O_LP, O_LS, O_P2 = range(6)
 
 
 def nt(a, b):
@@ -104,6 +103,7 @@
     sb_rcv,
     prev_snd,
     prev_rcv,
+    prev2_rcv,
     lp_snd,
     lp_rcv,
     ls_snd,
@@ -114,7 +114,9 @@
     out_b,
     out_p,
     g_acc,
+    g_part,
     g_rcv,
+    g_all,
     in_sem,
     do_sem,
     tab_sem,
@@ -146,18 +148,32 @@
     def _():
         pl.semaphore_signal(barrier, inc=1, device_id=right, device_id_type=MESH)
 
-    z_lo = me // 32
-    z_hi = dp // 2
-    place = lax.rem(me, 32)
-    other_half = [(k * 32 + place, (1 - z_hi) * 2 + lax.rem(dp, 2)) for k in range(4)]
-    same_half = [(lax.rem(z_lo + k, 4) * 32 + place, dp) for k in range(1, 4)]
-    for peer in groups[0] + groups[2] + same_half:
-        pl.semaphore_signal(barrier, inc=1, device_id=peer, device_id_type=MESH)
-
-    @pl.when(z_hi == 0)
-    def _():
-        for peer in other_half:
-            pl.semaphore_signal(barrier, inc=1, device_id=peer, device_id_type=MESH)
+    x = lax.rem(me // 8, 4)
+    y = lax.rem(me, 8)
+    z = (dp // 2) * 4 + me // 32
+    core = lax.rem(dp, 2)
+
+    def greet(sem, peer):
+        pl.semaphore_signal(sem, inc=1, device_id=peer, device_id_type=MESH)
+
+    def at(x_, z_, core_):
+        return (((z_ % 4) * 4 + x_) * 8 + y, (z_ // 4) * 2 + core_)
+
+    for peer in groups[0]:
+        greet(barrier, peer)
+    greet(barrier, (me, dp + 1 - 2 * core))
+    for k in range(8):
+
+        @pl.when(k > z)
+        def _():
+            greet(barrier, at(x, k, core))
+
+    for k in range(4):
+
+        @pl.when(k > x)
+        def _():
+            greet(barrier, (me + (k - x) * 8, dp))
+            greet(barrier, (me + (k - x) * 8, dp + 1 - 2 * core))
 
     def load_tables(h):
         return [
@@ -167,7 +183,7 @@
         ] + [
             pltpu.make_async_copy(
                 patch_ref.at[0, :, cols((part + 1) * HEADS + h)],
-                tabx.at[h, part, pl.ds(0, CAP)],
+                tabx.at[h, part],
                 tab_sem.at[h, part + 1],
             )
             for part in range(2)
@@ -207,6 +223,7 @@
         effs_l[...] = jnp.zeros_like(effs_l)
         dq_rcv[...] = jnp.zeros_like(dq_rcv)
         prev_rcv[...] = jnp.zeros_like(prev_rcv)
+        prev2_rcv[...] = jnp.zeros_like(prev2_rcv)
         sb_rcv[...] = jnp.full(sb_rcv.shape, NEG, F32)
 
     @pl.when(jnp.logical_not(has_right))
@@ -230,7 +247,7 @@
     def make_hidden(h, carry):
         for part in range(3):
             cb = part * HEADS + h
-            rows = nn(oh[...], tabq[h] if part == 0 else tabx[h, part - 1, :CAP])
+            rows = nn(oh[...], tabq[h] if part == 0 else tabx[h, part - 1])
             prev_snd[cb] = rows[ROWS - 1 : ROWS]
             hidden = gain_ref[:, cols(cb)] * rows + byte_v[:, cols(cb)].astype(F32)
             hidden_dst(part, h)[...] = hidden.astype(BF)
@@ -241,13 +258,21 @@
         load_do(h).wait()
 
     neighbours = has_left.astype(jnp.int32) + has_right.astype(jnp.int32)
-    pl.semaphore_wait(barrier, neighbours + 17 + 4 * z_hi)
-
-    @pl.when(z_hi == 1)
-    def _():
-        for peer in other_half:
-            pl.semaphore_signal(hi_sem, inc=1, device_id=peer, device_id_type=MESH)
-
+    pl.semaphore_wait(barrier, neighbours + 8 + z + 2 * x)
+
+    def answer():
+        for k in range(8):
+
+            @pl.when(k < z)
+            def _():
+                greet(hi_sem, at(x, k, core))
+
+        for k in range(4):
+
+            @pl.when(k < x)
+            def _():
+                greet(hi_sem, (me + (k - x) * 8, dp))
+                greet(hi_sem, (me + (k - x) * 8, dp + 1 - 2 * core))
 
     def remote(kind, h, src, dst, to):
         return pltpu.make_async_remote_copy(
@@ -299,6 +324,7 @@
     c_prev = once(O_PREV, prev_snd, prev_rcv, right)
     c_el = once(O_EL, effs, effs_r, left)
     c_er = once(O_ER, effs, effs_l, right)
+    c_p2 = once(O_P2, prev_rcv, prev2_rcv, right)
     c_lp = once(O_LP, lp_snd, lp_rcv, left)
     c_ls = once(O_LS, ls_snd, ls_rcv, left)
 
@@ -316,13 +342,9 @@
 
     lead_rows = lax.broadcasted_iota(jnp.int32, (16, HD), 0) < lead
 
-    first_row = lax.broadcasted_iota(jnp.int32, (EXT - CAP, HD), 0) == 0
-
     def fix_hidden(h, carry):
         for part in range(3):
             cb = part * HEADS + h
-            if part > 0:
-                tabx[h, part - 1, CAP:] = jnp.where(first_row, prev_rcv[cb], 0.0).astype(BF)
             dst = hidden_dst(part, h)
             fixed = gain_ref[:, cols(cb)] * prev_rcv[cb] + byte_v[:16, cols(cb)].astype(F32)
             dst[:16] = jnp.where(lead_rows, fixed, dst[:16].astype(F32)).astype(BF)
@@ -343,10 +365,16 @@
 
     for h in range(AHEAD):
         send_inputs(h, False)
+    answer()
+
+    @pl.when(has_right)
+    def _():
+        c_p2.start()
 
     @pl.when(has_left)
     def _():
         c_er.wait_recv()
+        c_p2.wait_recv()
 
     @pl.when(has_right)
     def _():
@@ -484,7 +512,7 @@
         ls_snd[h, 0:1] = sums[CAP : CAP + 1]
         sent = nn(mem_r[...], dq_snd[h])
         from_q[h, 0:1] = sent[CAP : CAP + 1]
-        g_acc[0, h] = (
+        g_acc[h] = (
             column_sum(sums[:CAP] * tabq[h].astype(F32))
             + sums[CAP : CAP + 1] * prev_rcv[h]
             + column_sum(sent[:CAP] * tabq_rcv[h].astype(F32))
@@ -496,9 +524,13 @@
             ls_snd[h, part + 1 : part + 2] = sums[CAP : CAP + 1]
             sent = nn(mem_l[...], dkv_snd[h, part])
             lp_snd[h, part : part + 1] = sent[CAP : CAP + 1]
-            g_acc[0, (part + 1) * HEADS + h] = column_sum(
-                sums * tabx[h, part].astype(F32)
-            ) + column_sum(sent * tabx_rcv[h, part].astype(F32))
+            cb = (part + 1) * HEADS + h
+            g_acc[cb] = (
+                column_sum(sums[:CAP] * tabx[h, part].astype(F32))
+                + sums[CAP : CAP + 1] * prev_rcv[cb]
+                + column_sum(sent[:CAP] * tabx_rcv[h, part].astype(F32))
+                + sent[CAP : CAP + 1] * prev2_rcv[cb]
+            )
         ls_snd[h, 3:4] = sums[CAP : CAP + 1]
 
     def out_byte(part, h):
@@ -579,7 +611,7 @@
         def _():
             phase2(s - LAG2)
 
-        @pl.when(jnp.logical_and(s >= FIRST, s < FIRST + FLIGHT))
+        @pl.when(jnp.logical_and(s >= FIRST, s < FIRST + SENT))
         def _():
             send_dkv(s - FIRST)
 
@@ -591,18 +623,32 @@
 
     lax.fori_loop(0, HEADS + LAG2, step, 0)
 
+    pos = x * 2 + core
+    stages = (groups[2], groups[0], groups[1], groups[2])
+
+    def share(p):
+        return pl.ds(p * 3, 3)
+
     def gain_copies(t):
-        return [
-            pltpu.make_async_remote_copy(
-                src_ref=g_acc.at[t],
-                dst_ref=g_rcv.at[t, k],
-                send_sem=gs_sem.at[t, k],
-                recv_sem=gr_sem.at[t, k],
-                device_id=peer,
-                device_id_type=MESH,
+        copies = []
+        for k, peer in enumerate(stages[t]):
+            if t == 0:
+                src, dst = g_acc.at[share(lax.rem(pos + k + 1, 8))], g_rcv.at[0, k]
+            elif t < 3:
+                src, dst = g_part.at[t - 1], g_rcv.at[t, k]
+            else:
+                src, dst = g_all.at[share(pos)], g_all.at[share(pos)]
+            copies.append(
+                pltpu.make_async_remote_copy(
+                    src_ref=src,
+                    dst_ref=dst,
+                    send_sem=gs_sem.at[t, k],
+                    recv_sem=gr_sem.at[t, k],
+                    device_id=peer,
+                    device_id_type=MESH,
+                )
             )
-            for k, peer in enumerate(groups[t])
-        ]
+        return copies
 
     def gain_start(t):
         for copy in gain_copies(t):
@@ -611,27 +657,35 @@
     def gain_finish(t):
         for copy in gain_copies(t):
             copy.wait_recv()
-        total = g_acc[t]
+        if t == 3:
+            gg_ref[...] = g_all[...] / ROWS
+            return
+        total = g_acc[share(pos)] if t == 0 else g_part[t - 1]
         for k in range(7):
             total = total + g_rcv[t, k]
         if t < 2:
-            g_acc[t + 1] = total
+            g_part[t] = total
         else:
-            gg_ref[...] = total / ROWS
+            g_all[share(pos)] = total
 
     def run_phase3(h, carry):
         phase3(h)
         return carry
 
     lax.fori_loop(0, HEADS, run_phase3, 0)
+    answers = 7 - z + 2 * (3 - x)
+
+    @pl.when(answers > 0)
+    def _():
+        pl.semaphore_wait(hi_sem, answers)
+
     gain_start(0)
 
     @pl.when(has_left)
     def _():
         c_lp.start()
 
-    for h in range(FLIGHT, HOLD):
-        send_dkv(h)
+    send_dkv(SENT)
     for h in range(HEADS + LAG2 - FIRST, HEADS):
         send_dq(h)
 
@@ -657,29 +711,28 @@
 
     for h in range(HEADS):
         results(h)
+        if h == 0:
+            gain_finish(0)
+            gain_start(1)
+            for g in range(SENT + 1, 6):
+                send_dkv(g)
         if h == 1:
             forward_lead()
-            for g in range(HOLD, HEADS):
+            for g in range(6, HEADS):
                 send_dkv(g)
-        if h == 2:
-            gain_finish(0)
-
-            @pl.when(z_hi == 0)
-            def _():
-                pl.semaphore_wait(hi_sem, 4)
-
-            gain_start(1)
-        if h == 4:
+        if h == 3:
             gain_finish(1)
             gain_start(2)
-        if h == 6:
+        if h == 5:
+            gain_finish(2)
+            gain_start(3)
             take_lead()
-            for g in range(6):
+            for g in range(5):
                 patch_results(g)
-            gain_finish(2)
-        if h >= 6:
+        if h >= 5:
             patch_results(h)
-    for t in range(3):
+    gain_finish(3)
+    for t in range(4):
         for copy in gain_copies(t):
             copy.wait_send()
 
@@ -708,8 +761,36 @@
 
     @pl.when(has_right)
     def _():
-        for copy in (c_prev, c_er):
+        for copy in (c_prev, c_er, c_p2):
             copy.wait_send()
+
+
+CHUNKS = 8
+
+
+def place(byte_in, patch_in, gain_in, byte_out, patch_out, gain_out, byte_v, patch_v, gain_v, sem):
+    rows = ROWS // CHUNKS
+    moves = [
+        (
+            byte_in.at[0, pl.ds(k * rows, rows)],
+            byte_v.at[pl.ds(k * rows, rows)],
+            byte_out.at[0, pl.ds(k * rows, rows)],
+        )
+        for k in range(CHUNKS)
+    ] + [(patch_in, patch_v, patch_out), (gain_in, gain_v, gain_out)]
+    loads = [
+        pltpu.make_async_copy(src, mid, sem.at[0, k]) for k, (src, mid, _) in enumerate(moves)
+    ]
+    stores = [
+        pltpu.make_async_copy(mid, dst, sem.at[1, k]) for k, (_, mid, dst) in enumerate(moves)
+    ]
+    for load in loads:
+        load.start()
+    for load, store in zip(loads, stores):
+        load.wait()
+        store.start()
+    for store in stores:
+        store.wait()
 
 
 def local(byte_qkv, patch_qkv, patch_gain, out_grad, patch_slot, lead):
@@ -730,9 +811,9 @@
         scratch_shapes=[
             V((ROWS, width), BF),
             V((HEADS, CAP, HD), BF),
-            V((HEADS, 2, EXT, HD), BF),
+            V((HEADS, 2, CAP, HD), BF),
             V((HEADS, CAP, HD), BF),
-            V((HEADS, 2, EXT, HD), BF),
+            V((HEADS, 2, CAP, HD), BF),
             V((ROWS, CAP), BF),
             V((EXT, ROWS), BF),
             V((EXT, ROWS), BF),
@@ -758,6 +839,7 @@
             V((HEADS, 4, ROWS), F32),
             V((3 * HEADS, 1, HD), F32),
             V((3 * HEADS, 1, HD), F32),
+            V((3 * HEADS, 1, HD), F32),
             V((HEADS, 2, HD), F32),
             V((HEADS, 2, HD), F32),
             V((HEADS, 4, HD), F32),
@@ -767,25 +849,44 @@
             V((HEADS, 3, CAP, HD), F32),
             V((HEADS, 3, ROWS, HD), BF),
             V((HEADS, 3, CAP, HD), BF),
-            V((3, 3 * HEADS, 1, HD), F32),
-            V((3, 7, 3 * HEADS, 1, HD), F32),
+            V((3 * HEADS, 1, HD), F32),
+            V((2, 3, 1, HD), F32),
+            V((3, 7, 3, 1, HD), F32),
+            V((3 * HEADS, 1, HD), F32),
             pltpu.SemaphoreType.DMA((1,)),
             pltpu.SemaphoreType.DMA((HEADS,)),
             pltpu.SemaphoreType.DMA((HEADS, 3)),
             pltpu.SemaphoreType.DMA((9, HEADS)),
             pltpu.SemaphoreType.DMA((9, HEADS)),
-            pltpu.SemaphoreType.DMA((5,)),
-            pltpu.SemaphoreType.DMA((5,)),
+            pltpu.SemaphoreType.DMA((6,)),
+            pltpu.SemaphoreType.DMA((6,)),
             pltpu.SemaphoreType.REGULAR,
             pltpu.SemaphoreType.DMA((HEADS, 3)),
             pltpu.SemaphoreType.DMA((HEADS, 3)),
-            pltpu.SemaphoreType.DMA((3, 7)),
-            pltpu.SemaphoreType.DMA((3, 7)),
+            pltpu.SemaphoreType.DMA((4, 7)),
+            pltpu.SemaphoreType.DMA((4, 7)),
         ],
         compiler_params=pltpu.CompilerParams(
             collective_id=0, has_side_effects=True, vmem_limit_bytes=62 * 2**20
         ),
     )(byte_qkv, patch_qkv, patch_gain.reshape(1, width), out_grad, patch_slot, lead)
+    byte_grad, patch_grad, gain_grad = pl.pallas_call(
+        place,
+        out_shape=(
+            jax.ShapeDtypeStruct((1, ROWS, width), BF),
+            jax.ShapeDtypeStruct((1, CAP, width), BF),
+            jax.ShapeDtypeStruct((3 * HEADS, 1, HD), F32),
+        ),
+        in_specs=[any_spec] * 3,
+        out_specs=(any_spec,) * 3,
+        scratch_shapes=[
+            V((ROWS, width), BF),
+            V((1, CAP, width), BF),
+            V((3 * HEADS, 1, HD), F32),
+            pltpu.SemaphoreType.DMA((2, CHUNKS + 2)),
+        ],
+        compiler_params=pltpu.CompilerParams(vmem_limit_bytes=62 * 2**20),
+    )(byte_grad, patch_grad, gain_grad)
     return byte_grad, patch_grad, gain_grad.reshape(width)
 
 

time: 82.8 us -> 78.8 us (0.952)
  the two profiles are of different devices: /device:TPU:125 before, /device:TPU:1 now
where the time goes in v3:
time: 78.8 us; the launch traced here: 78.5 us
  Pallas kernels  77.2 us (98%)
  between operations  1.29 us (2%)
    pallas_call x1, Pallas kernels, local(): pl.pallas_call(kernel, out_shape=(jax.ShapeDtypeStruct((1, ROWS, width),...  74.7 us
    pallas_call x1, Pallas kernels, local(): pl.pallas_call(place, out_shape=(jax.ShapeDtypeStruct((1, ROWS, width), B...  2.51 us

profile of v3, /device:TPU:1, one launch (start us, length us, event | category | flops | bytes accessed | tf_op | source)
XLA Modules:
  0.0 78.5 jit_solution(13557367186479227030)
XLA Ops:
  1.3 74.7 %shard_map.85 = (bf16[1,256,3072]{2,1,0:T(8,128)(2,1)}, bf16[1,64,3072]{2,1,0:T(8,128)(2,1)}, f32[24,1,128]{2,1,0:T(1,128)}) custom-call(bf16[1,256,3072]{2,1,0:T(8,128)(2,1)} %byte_ref.1, bf16[1,64,3072]{2,1,0:T(8,128)(2,1)} %patch_ref.1, f32[1,3072]{1,0:T(1,128)} %bitcast.2, bf16[1,256,1024]{2,1,0:T(8,128)(2,1)} %cot_ref.1, s32[1,256]{1,0:T(1,128)} %slot_ref.1, ...), custom_call_target="tpu_custom_call" | custom-call | tf_op jit(solution)/shard_map/pallas_call | solution.py:802
  76.0 2.5 %shard_map.86 = (bf16[1,256,3072]{2,1,0:T(8,128)(2,1)}, bf16[1,64,3072]{2,1,0:T(8,128)(2,1)}, f32[24,1,128]{2,1,0:T(1,128)}) custom-call(bf16[1,256,3072]{2,1,0:T(8,128)(2,1)} %get-tuple-element.9.byte_in, bf16[1,64,3072]{2,1,0:T(8,128)(2,1)} %get-tuple-element.10.patch_in, f32[24,1,128]{2,1,0:T(1,128)} %get-tuple-element.11.gain_in), custom_call_target="tpu_custom_call" | custom-call | tf_op jit(solution)/shard_map/pallas_call | solution.py:873
